TPU v7x, 32 devices: a whole 2x2x4 slice. The times are simulated.
32 devices in a mesh: parts: 2 (over y), tensor: 4 (over z), dp: 4 (over x, core).
Axes of the slice: x: 2, y: 2, z: 4, core: 2. Of those that a mesh axis runs over, the one named last changes fastest.
Arguments:
- activations: bfloat16 [64, 120, 8192], P(('parts', 'dp'), None, 'tensor'), parts along dimension 0, may hold values from -6 to 6
- frozen_weight: bfloat16 [8192, 2048], P('tensor'), may hold values from -0.09375 to 0.09375
- cotangent: bfloat16 [64, 120, 2048], P(('parts', 'dp'), None, 'tensor'), parts along dimension 0, may hold values from -6 to 6
- adapter_down_weight: bfloat16 [256, 16, 8192], P(('parts', 'dp'), None, 'tensor'), parts along dimension 0, may hold values from -0.0625 to 0.0625
- adapter_up_weight: bfloat16 [256, 16, 2048], P(('parts', 'dp'), None, 'tensor'), parts along dimension 0, may hold values from -1.5 to 1.5
- sequence_adapter: int32 [64], P('parts'), parts along dimension 0, may hold values from 0 to 127, as said below
- adapter_store_row: int32 [256], P('parts'), parts along dimension 0, may hold values from 0 to 127, as said below
- group_live_counts: int32 [8], P(('parts', 'dp')), parts along dimension 0, may hold values from 1 to 8, as said below
Outputs:
- key_value_output: bfloat16 [64, 120, 2048], P(('parts', 'dp'), None, 'tensor'), parts along dimension 0
- grad_input: bfloat16 [64, 120, 8192], P(('parts', 'dp'), None, 'tensor'), parts along dimension 0
- grad_down: float32 [256, 16, 8192], P(('parts', 'dp'), None, 'tensor'), parts along dimension 0
- grad_up: float32 [256, 16, 2048], P(('parts', 'dp'), None, 'tensor'), parts along dimension 0
There are 2 independent parts, one for each index of `parts`. A program takes and returns all parts, laid end to end along the dimension named above; an argument that names none is the same for every part. Nothing has to cross between parts.
Inputs may be any that keep to these rules, and one draw needn't show every extreme that they name: `adapter_store_row`: A permutation: each store row holds one adapter. Store rows g * 32 to (g + 1) * 32 - 1 lie on index g of dp. `sequence_adapter`: among the 8 slots of one data group, at most 2 use adapters whose store rows lie on one index of dp, and every group reaches 2 for some index. Slots may share an adapter. `group_live_counts`: live slots of a group come first. Some group is full and some group has one live sequence.
All inputs are finite; a program needn't handle non-finite values.
Results may differ from a plain program's by a relative error of at most 0.013.
Values may be sent and summed in bfloat16 or wider, within the bound.
A program may use at most 128 MiB of HBM per device.

v0:
```python
import jax
import jax.numpy as jnp
from jax import lax
from jax.sharding import PartitionSpec as P

CAP_OWN = 2


adapter_scale = 2.0


def shards(
    activations,
    frozen_weight,
    cotangent,
    adapter_down_weight,
    adapter_up_weight,
    sequence_adapter,
    adapter_store_row,
    group_live_counts,
):
    group_total = lax.axis_size("dp")
    slot_count, seq_length, dim_shard = activations.shape
    holder_count = adapter_down_weight.shape[0]
    output_portion = adapter_up_weight.shape[2]
    full_out = frozen_weight.shape[1]
    group_index = lax.axis_index("dp")
    tensor_index = lax.axis_index("tensor")
    capacity = CAP_OWN
    adapter_rows = adapter_store_row[sequence_adapter]
    owners = (adapter_rows // holder_count).reshape(group_total, slot_count)
    local_rows = (adapter_rows % holder_count).reshape(group_total, slot_count)
    slot_ids = jnp.arange(slot_count, dtype=jnp.int32)
    same_owner = owners[:, :, None] == owners[:, None, :]
    earlier_slot = slot_ids[None, :] < slot_ids[:, None]
    owner_rank = jnp.sum((same_owner & earlier_slot[None]).astype(jnp.int32), axis=2)
    cap_ids = jnp.arange(capacity, dtype=jnp.int32)
    owner_hits = (
        (owners == group_index)[:, :, None] & (owner_rank[:, :, None] == cap_ids[None, None, :])
    ).astype(jnp.float32)
    local_match = (
        local_rows[:, :, None] == jnp.arange(holder_count, dtype=jnp.int32)[None, None, :]
    ).astype(jnp.float32)
    selection = jnp.einsum("ejc,ejk->eck", owner_hits, local_match)
    mine_owner = lax.dynamic_index_in_dim(owners, group_index, 0, keepdims=False)
    mine_rank = lax.dynamic_index_in_dim(owner_rank, group_index, 0, keepdims=False)
    group_ids = jnp.arange(group_total, dtype=jnp.int32)
    pick_table = (
        (mine_owner[:, None] == group_ids[None, :])[:, :, None]
        & (mine_rank[:, None] == cap_ids[None, :])[:, None, :]
    ).astype(jnp.float32)
    live_sequence_mask = (slot_ids < group_live_counts[0]).astype(jnp.bfloat16)[:, None, None]
    every_down, every_up = (
        lax.all_gather(adapter_down_weight, "dp", axis=0, tiled=True),
        lax.all_gather(adapter_up_weight, "dp", axis=0, tiled=True),
    )
    mine_rows = lax.dynamic_slice_in_dim(adapter_rows, group_index * slot_count, slot_count)
    one_hot = (
        mine_rows[:, None] == jnp.arange(group_total * holder_count, dtype=jnp.int32)[None, :]
    ).astype(jnp.bfloat16)
    down_weight_slice = jnp.einsum(
        "ja,ard->jrd", one_hot, every_down, preferred_element_type=jnp.float32
    ).astype(jnp.bfloat16)
    up_weight_slice = jnp.einsum(
        "ja,arw->jrw", one_hot, every_up, preferred_element_type=jnp.float32
    ).astype(jnp.bfloat16)
    low_sum = lax.psum(
        jnp.einsum(
            "cfy,cjy->cfj", activations, down_weight_slice, preferred_element_type=jnp.float32
        ).astype(jnp.bfloat16),
        "tensor",
    )
    partial_value = jnp.dot(
        activations.reshape(slot_count * seq_length, dim_shard),
        frozen_weight,
        preferred_element_type=jnp.float32,
    ).reshape(slot_count, seq_length, full_out)
    whole_sum = lax.psum(partial_value.astype(jnp.bfloat16), "tensor").astype(jnp.float32)
    frozen_output = lax.dynamic_slice_in_dim(
        whole_sum, tensor_index * output_portion, output_portion, 2
    )
    live_mask_float = live_sequence_mask.astype(jnp.float32)
    adapter_contribution = jnp.einsum(
        "slr,srw->slw", low_sum, up_weight_slice, preferred_element_type=jnp.float32
    )
    key_value_output = (
        (frozen_output + adapter_scale * adapter_contribution) * live_mask_float
    ).astype(jnp.bfloat16)
    masked = cotangent * live_sequence_mask
    masked_full = lax.all_gather(masked, "tensor", axis=2, tiled=True)
    back_sum = lax.psum(
        (
            adapter_scale
            * jnp.einsum(
                "bvg,bqg->bvq", masked, up_weight_slice, preferred_element_type=jnp.float32
            )
        ).astype(jnp.bfloat16),
        "tensor",
    )
    frozen_path = lax.dot_general(
        masked_full.reshape(slot_count * seq_length, full_out),
        frozen_weight,
        (((1,), (1,)), ((), ())),
        preferred_element_type=jnp.float32,
    )
    input_gradient = frozen_path.reshape(slot_count, seq_length, dim_shard) + jnp.einsum(
        "qip,qpb->qib", back_sum, down_weight_slice, preferred_element_type=jnp.float32
    )
    grad_input = (input_gradient * live_mask_float).astype(jnp.bfloat16)
    down_contributions = jnp.einsum(
        "ihn,ihx->inx", back_sum, activations, preferred_element_type=jnp.float32
    )
    up_contributions = adapter_scale * jnp.einsum(
        "tun,tuq->tnq", low_sum, masked, preferred_element_type=jnp.float32
    )
    send_grad_down = jnp.einsum(
        "joc,jrd->ocrd", pick_table, down_contributions, precision=lax.Precision.HIGHEST
    )
    send_grad_up = jnp.einsum(
        "joc,jrw->ocrw", pick_table, up_contributions, precision=lax.Precision.HIGHEST
    )
    back_down, back_up = (
        lax.all_to_all(
            send_grad_down.astype(jnp.bfloat16), "dp", split_axis=0, concat_axis=0, tiled=True
        ).astype(send_grad_down.dtype),
        lax.all_to_all(
            send_grad_up.astype(jnp.bfloat16), "dp", split_axis=0, concat_axis=0, tiled=True
        ).astype(send_grad_up.dtype),
    )
    grad_down = jnp.einsum("eck,ecrd->krd", selection, back_down, precision=lax.Precision.HIGHEST)
    grad_up = jnp.einsum("eck,ecrw->krw", selection, back_up, precision=lax.Precision.HIGHEST)
    return (key_value_output, grad_input, grad_down, grad_up)


def solution(mesh):
    in_specs = (
        P(("parts", "dp"), None, "tensor"),
        P("tensor", None),
        P(("parts", "dp"), None, "tensor"),
        P(("parts", "dp"), None, "tensor"),
        P(("parts", "dp"), None, "tensor"),
        P("parts"),
        P("parts"),
        P(("parts", "dp")),
    )
    out_specs = (
        P(("parts", "dp"), None, "tensor"),
        P(("parts", "dp"), None, "tensor"),
        P(("parts", "dp"), None, "tensor"),
        P(("parts", "dp"), None, "tensor"),
    )
    return jax.shard_map(shards, mesh=mesh, in_specs=in_specs, out_specs=out_specs, check_vma=False)
```

profile of v0, /device:TPU:0, one launch (start us, length us, event | category | flops | bytes accessed | tf_op | source)
XLA Modules:
  0.0 343.0 jit_solution(12266888204056100460)
XLA Ops:
  7.2 0.0 copy-start
  7.2 0.0 copy-start.4
  7.2 0.0 all-gather.6.cloned.1.call-start
  7.2 2.3 copy.48
  9.5 0.0 all-gather.6.cloned.1.call-update
  9.5 0.0 all-gather.8.cloned.1.call-start
  10.2 2.3 broadcast_multiply_fusion
  12.5 0.0 all-gather.8.cloned.1.call-update
  12.5 0.0 all-gather.4.cloned.1.call-start
  12.6 0.0 copy-done.4
  12.6 2.5 copy.46
  15.1 0.0 all-gather.4.cloned.1.call-update
  15.1 0.0 all-reduce.3.cloned.1.call-start
  15.2 13.1 %fusion.4 = bf16[8,120,2048]{2,1,0:T(8,128)(2,1)} fusion(bf16[8,120,2048]{2,1,0:T(8,128)(2,1)} %param.8, bf16[2048,2048]{1,0:T(8,128)(2,1)} %param.9), kind=kOutput, calls=%fused_computation.6 | convolution fusion | flops 8055029760 | bytes 16252928 | tf_op jit(solution)/shard_map/dot_general | solution.py:73
  28.3 0.0 copy-start.5
  28.3 0.0 copy-start.3
  28.3 0.0 all-reduce.3.cloned.1.call-update
  28.3 0.6 copy-done.5
  29.0 0.0 copy-done
  29.0 0.7 gather_fusion
  29.7 0.1 gather.6
  29.8 0.1 dynamic_slice.14
  29.9 0.2 convert_reduce_fusion
  30.1 0.2 convolution_bitcast_fusion.3
  30.3 5.2 %all-gather.6.cloned.1.call-done = bf16[128,16,512]{2,0,1:T(8,128)(2,1)} async-done(((bf16[32,16,512]{2,0,1:T(8,128)(2,1)}), bf16[128,16,512]{2,0,1:T(8,128)(2,1)}) %all-gather.6.cloned.1.call-update) | async-done | bytes 2097168 | tf_op jit(solution)/shard_map/all_gather | solution.py:55
  35.5 2.0 convolution_convert_fusion.3
  37.5 0.0 copy-done.3
  37.5 0.4 fusion.8
  37.9 76.2 %all-gather.8.cloned.1.call-done = bf16[8,120,2048]{2,1,0:T(8,128)(2,1)} async-done(((bf16[8,120,512]{2,1,0:T(8,128)(2,1)}), bf16[8,120,2048]{2,1,0:T(8,128)(2,1)}) %all-gather.8.cloned.1.call-update) | async-done | bytes 3932176 | tf_op jit(solution)/shard_map/all_gather | solution.py:90
  114.1 13.9 %fusion = f32[8,120,2048]{2,1,0:T(8,128)} fusion(bf16[8,120,2048]{2,1,0:T(8,128)(2,1)} %all-gather.8.cloned.1.call-done, bf16[2048,2048]{1,0:T(8,128)(2,1)} %param.9), kind=kOutput, calls=%fused_computation.1 | convolution fusion | flops 8053063680 | bytes 20185088 | tf_op jit(solution)/shard_map/dot_general | solution.py:100
  128.0 45.1 %all-gather.4.cloned.1.call-done = bf16[128,16,2048]{2,0,1:T(8,128)(2,1)} async-done(((bf16[32,16,2048]{2,0,1:T(8,128)(2,1)}), bf16[128,16,2048]{2,0,1:T(8,128)(2,1)}) %all-gather.4.cloned.1.call-update) | async-done | bytes 8388624 | tf_op jit(solution)/shard_map/all_gather | solution.py:54
  173.1 0.0 copy-start.2
  173.1 4.8 %convolution_convert_fusion.1 = bf16[8,16,2048]{2,0,1:T(8,128)(2,1)S(1)} fusion(bf16[128,16,2048]{2,0,1:T(8,128)(2,1)} %all-gather.4.cloned.1.call-done, s32[8]{0:T(128)S(1)} %dynamic_slice.14), kind=kOutput, calls=%fused_computation.10 | convolution fusion | flops 67372032 | bytes 8912928 | tf_op jit(solution)/shard_map/ja,ard->jrd/dot_general | solution.py:61
  177.9 0.0 copy-done.2
  177.9 1.2 fusion.9
  179.1 21.7 %all-reduce = (bf16[8,120,16]{1,2,0:T(8,128)(2,1)S(1)}, bf16[8,120,16]{1,2,0:T(8,128)(2,1)S(1)}) all-reduce(bf16[8,120,16]{1,2,0:T(8,128)(2,1)S(1)} %fusion.9, bf16[8,120,16]{1,2,0:T(8,128)(2,1)S(1)} %fusion.8), channel_id=1, replica_groups=mesh['parts'=2,'tensor'=4,'dp'=4] {'tensor'}, use_global_device_ids=true, to_apply=%region_1.2 | all-reduce | flops 30720 | bytes 122880 | tf_op jit(solution)/shard_map/psum | solution.py:67
  200.8 0.2 fusion.7
  201.0 0.4 convolution_convert_fusion.2
  201.4 0.8 copy.56
  202.2 3.3 all-to-all-start.1
  205.5 2.9 convolution_bitcast_fusion.1
  208.4 6.7 %multiply_convert_fusion = bf16[8,120,2048]{2,1,0:T(8,128)(2,1)} fusion(f32[8,120,2048]{2,1,0:T(8,128)} %fusion, bf16[8,120,16]{1,2,0:T(8,128)(2,1)S(1)} %get-tuple-element.21, f32[8]{0:T(128)S(1)} %fusion.36, bf16[8,16,2048]{2,0,1:T(8,128)(2,1)S(1)} %convolution_convert_fusion.1), kind=kOutput, calls=%fused_computation.5 | convolution fusion | flops 68812800 | bytes 12351520 | tf_op jit(solution)/shard_map/qip,qpb->qib/dot_general | solution.py:106
  215.1 1.4 convolution_convert_fusion
  216.6 1.3 copy.53
  217.9 0.0 all-to-all-done.1
  217.9 3.5 %all-to-all-start = ((bf16[4,2,16,2048]{3,1,2,0:T(2,128)(2,1)}), bf16[4,2,16,2048]{3,1,2,0:T(2,128)(2,1)S(1)}, u32[]{:S(2)}, u32[]{:S(2)}) async-start(bf16[4,2,16,2048]{3,1,2,0:T(2,128)(2,1)} %copy.53), calls=%async_computation | async-start | bytes 1048576 | tf_op jit(solution)/shard_map/all_to_all | solution.py:123
  221.4 103.0 %all-reduce.3.cloned.1.call-done = bf16[8,120,2048]{2,1,0:T(8,128)(2,1)} async-done(((bf16[8,120,2048]{2,1,0:T(8,128)(2,1)}), bf16[8,120,2048]{2,1,0:T(8,128)(2,1)}) %all-reduce.3.cloned.1.call-update) | async-done | bytes 3932176 | tf_op jit(solution)/shard_map/psum | solution.py:78
  324.4 2.7 multiply_convert_fusion.1
  327.0 0.7 convolution_bitcast_fusion.2
  327.7 1.6 copy.59
  329.3 0.0 all-to-all-done
  329.3 0.0 copy-start.1
  329.3 2.6 convolution_bitcast_fusion
  332.0 4.4 %copy.58 = f32[32,16,2048]{2,1,0:T(8,128)} copy(f32[32,16,2048]{2,0,1:T(8,128)S(1)} %convolution_bitcast_fusion) | data formatting | bytes 8388608
  336.4 0.0 copy-done.1
  (10 shorter events, 0.1 us)
Async XLA Ops:
  7.2 21.8 %copy-start = (s32[128]{0:T(128)S(1)}, s32[128]{0:T(128)}, u32[]{:S(2)}) copy-start(s32[128]{0:T(128)} %param.14) | copy-start | bytes 1540
  7.2 5.4 %copy-start.4 = (bf16[32,16,2048]{2,1,0:T(8,128)(2,1)S(1)}, bf16[32,16,2048]{2,1,0:T(8,128)(2,1)}, u32[]{:S(2)}) copy-start(bf16[32,16,2048]{2,1,0:T(8,128)(2,1)} %param.11) | copy-start | bytes 6291460
  7.2 28.3 %all-gather.6.cloned.1.call-start = ((), (), s32[]{:S(2)}) async-start(), calls=%async_computation.4 | async-start | bytes 2621440 | tf_op jit(solution)/shard_map/all_gather | solution.py:55
  9.5 104.6 %all-gather.8.cloned.1.call-start = ((), (), s32[]{:S(2)}) async-start(), calls=%async_computation.5 | async-start | bytes 4915200 | tf_op jit(solution)/shard_map/all_gather | solution.py:90
  12.5 160.6 %all-gather.4.cloned.1.call-start = ((), (), s32[]{:S(2)}) async-start(), calls=%async_computation.3 | async-start | bytes 10485760 | tf_op jit(solution)/shard_map/all_gather | solution.py:54
  15.1 309.3 %all-reduce.3.cloned.1.call-start = ((), (), s32[]{:S(2)}) async-start(), calls=%async_computation.2 | async-start | bytes 7864320 | tf_op jit(solution)/shard_map/psum | solution.py:78
  28.3 0.7 copy-start.5
  28.3 9.2 %copy-start.3 = (bf16[8,120,512]{2,1,0:T(8,128)(2,1)S(1)}, bf16[8,120,512]{2,1,0:T(8,128)(2,1)}, u32[]{:S(2)}) copy-start(bf16[8,120,512]{2,1,0:T(8,128)(2,1)} %broadcast_multiply_fusion) | copy-start | bytes 2949124
  173.1 4.8 %copy-start.2 = (bf16[8,120,2048]{2,1,0:T(8,128)(2,1)S(1)}, bf16[8,120,2048]{2,1,0:T(8,128)(2,1)}, u32[]{:S(2)}) copy-start(bf16[8,120,2048]{2,1,0:T(8,128)(2,1)} %param.8) | copy-start | bytes 11796484
  202.2 15.7 %all-to-all-start.1 = ((bf16[4,2,16,512]{3,1,2,0:T(2,128)(2,1)}), bf16[4,2,16,512]{3,1,2,0:T(2,128)(2,1)S(1)}, u32[]{:S(2)}, u32[]{:S(2)}) async-start(bf16[4,2,16,512]{3,1,2,0:T(2,128)(2,1)} %copy.56), calls=%async_computation.1 | async-start | bytes 262144 | tf_op jit(solution)/shard_map/all_to_all | solution.py:126
  217.9 111.4 %all-to-all-start = ((bf16[4,2,16,2048]{3,1,2,0:T(2,128)(2,1)}), bf16[4,2,16,2048]{3,1,2,0:T(2,128)(2,1)S(1)}, u32[]{:S(2)}, u32[]{:S(2)}) async-start(bf16[4,2,16,2048]{3,1,2,0:T(2,128)(2,1)} %copy.53), calls=%async_computation | async-start | bytes 1048576 | tf_op jit(solution)/shard_map/all_to_all | solution.py:123
  329.3 7.1 %copy-start.1 = (s32[128]{0:T(128)S(1)}, s32[128]{0:T(128)}, u32[]{:S(2)}) copy-start(s32[128]{0:T(128)} %param.14) | copy-start | bytes 1540
Sparse Core Ops, SparseCore 0:
  10.2 25.2 all-gather.5
  37.6 76.4 all-gather.7
  116.2 56.8 all-gather.3
  175.9 148.3 all-reduce.2
where the time goes:
time: 343 us
  waiting for transfers between devices  230 us (67%)
  matrix products  53.3 us (16%)
  blocking collectives  21.7 us (6%)
  between operations  14.6 us (4%)
  local copies, waits for them, and re-layouts  14.4 us (4%)
  starting transfers between devices  6.96 us (2%)
    psum x1, waiting for transfers between devices, shards(): lax.psum(partial_value.astype(jnp.bfloat16), 'tensor').astype(jnp.float32)  103 us
    all_gather x1, waiting for transfers between devices, shards(): masked_full = lax.all_gather(masked, 'tensor', axis=2, tiled=True)  76.2 us
    all_gather x1, waiting for transfers between devices, shards(): lax.all_gather(adapter_down_weight, 'dp', axis=0, tiled=True)  45.1 us
    psum x1, blocking collectives, shards(): lax.psum(jnp.einsum('cfy,cjy->cfj', activations, down_weight_slice, prefe...  21.7 us
    dot_general x1, matrix products, shards(): lax.dot_general(masked_full.reshape(slot_count * seq_length, full_out), f...  13.9 us
    dot_general x1, matrix products, shards(): jnp.dot(activations.reshape(slot_count * seq_length, dim_shard), frozen_w...  13.1 us
    unnamed x16, local copies, waits for them, and re-layouts  11.4 us
  transfers between devices with their start and end apart: 6, of which 4 were waited for; matrix products, arithmetic and copies ran while one was open for 18% of the time, Pallas kernels for 0%

commit v1 on v0

--- a/solution.py
+++ b/solution.py
@@ -1,12 +1,335 @@
+import functools
+
 import jax
 import jax.numpy as jnp
 from jax import lax
+from jax.experimental import pallas as pl
+from jax.experimental.pallas import tpu as pltpu
 from jax.sharding import PartitionSpec as P
 
 CAP_OWN = 2
 
 
 adapter_scale = 2.0
+
+
+CHUNKS = 4
+MESH = pl.DeviceIdType.MESH
+NT = (((1,), (1,)), ((), ()))
+TN = (((0,), (0,)), ((), ()))
+
+
+def line_kernel(
+    n, chunks, slots,
+    x_hbm, w_hbm, cot_ref, alive_ref, down_ref, up_ref,
+    kv_ref, gin_ref, gdown_ref, gup_ref,
+    x_ref, w_ref, full, part, from_left, from_right, acc, small, lowt, backt,
+    load_sem, ag_recv, ag_right, ag_left, rs_recv_r, rs_recv_l, rs_send_r, rs_send_l,
+    small_send, small_recv,
+):
+    me = lax.axis_index("tensor")
+    rows, width = cot_ref.shape
+    depth = x_ref.shape[1]
+    rank = small.shape[1] // 2
+    size = rows // chunks
+    length = rows // slots
+    last = n - 1
+    mirror = last - me
+
+    def chunk(c):
+        return pl.ds(pl.multiple_of(c * size, size), size)
+
+    def columns(d):
+        return pl.ds(pl.multiple_of(d * width, width), width)
+
+    def ag_copy(b, c, to_right):
+        return pltpu.make_async_remote_copy(
+            src_ref=full.at[b, chunk(c)],
+            dst_ref=full.at[b, chunk(c)],
+            send_sem=(ag_right if to_right else ag_left).at[b, c],
+            recv_sem=ag_recv.at[b, c],
+            device_id={"tensor": me + 1 if to_right else me - 1},
+            device_id_type=MESH,
+        )
+
+    def rs_copy(d, c, to_right):
+        return pltpu.make_async_remote_copy(
+            src_ref=part.at[d, chunk(c)],
+            dst_ref=(from_left if to_right else from_right).at[d, chunk(c)],
+            send_sem=(rs_send_r if to_right else rs_send_l).at[d, c],
+            recv_sem=(rs_recv_r if to_right else rs_recv_l).at[d, c],
+            device_id={"tensor": me + 1 if to_right else me - 1},
+            device_id_type=MESH,
+        )
+
+    def small_copy(peer, slot):
+        return pltpu.make_async_remote_copy(
+            src_ref=small.at[slot],
+            dst_ref=small.at[slot],
+            send_sem=small_send.at[peer],
+            recv_sem=small_recv.at[slot],
+            device_id={"tensor": peer},
+            device_id_type=MESH,
+        )
+
+    load_x = pltpu.make_async_copy(x_hbm, x_ref, load_sem.at[0])
+    load_w = pltpu.make_async_copy(w_hbm, w_ref, load_sem.at[1])
+    load_x.start()
+    load_w.start()
+    barrier = pltpu.get_barrier_semaphore()
+    for step in range(1, n):
+        pl.semaphore_signal(
+            barrier, inc=1, device_id={"tensor": lax.rem(me + step, n)}, device_id_type=MESH
+        )
+    full[me] = (cot_ref[...].astype(jnp.float32) * alive_ref[...]).astype(full.dtype)
+    pl.semaphore_wait(barrier, n - 1)
+
+    @pl.loop(0, chunks)
+    def _(c):
+        @pl.when(me < last)
+        def _():
+            ag_copy(me, c, True).start()
+
+        @pl.when(me > 0)
+        def _():
+            ag_copy(me, c, False).start()
+
+    shape = (slots * rank, rows)
+    slot_of_row = lax.broadcasted_iota(jnp.int32, shape, 0) // rank
+    slot_of_column = lax.broadcasted_iota(jnp.int32, shape, 1) // length
+    diagonal = slot_of_row == slot_of_column
+
+    def compact(wide):
+        wide = jnp.where(diagonal, wide, 0.0)
+        total = wide[0:rank]
+        for s in range(1, slots):
+            total = total + wide[s * rank : (s + 1) * rank]
+        return total
+
+    back_part = compact(
+        lax.dot_general(up_ref[...], full[me], NT, preferred_element_type=jnp.float32)
+    )
+    small[me, rank:, :] = (adapter_scale * back_part).astype(small.dtype)
+    load_x.wait()
+    low_part = compact(
+        lax.dot_general(down_ref[...], x_ref[...], NT, preferred_element_type=jnp.float32)
+    )
+    small[me, :rank, :] = low_part.astype(small.dtype)
+    for step in range(1, n):
+        small_copy(lax.rem(me + step, n), me).start()
+    load_w.wait()
+
+    @pl.loop(0, n)
+    def _(k):
+        d = jnp.where(me == 0, last - k, k)
+
+        @pl.loop(0, chunks)
+        def _(c):
+            part[d, chunk(c), :] = jnp.dot(
+                x_ref[chunk(c), :], w_ref[:, columns(d)], preferred_element_type=jnp.float32
+            ).astype(part.dtype)
+
+            @pl.when((me == 0) & (d > 0))
+            def _():
+                rs_copy(d, c, True).start()
+
+            @pl.when((me == last) & (d < last))
+            def _():
+                rs_copy(d, c, False).start()
+
+    def frozen(b, first):
+        @pl.loop(0, chunks)
+        def _(c):
+            @pl.loop(0, depth // width)
+            def _(j):
+                piece = lax.dot_general(
+                    full[b, chunk(c), :],
+                    w_ref[columns(j), columns(b)],
+                    NT,
+                    preferred_element_type=jnp.float32,
+                )
+                if first:
+                    acc[chunk(c), columns(j)] = piece
+                else:
+                    acc[chunk(c), columns(j)] += piece
+
+    frozen(me, True)
+
+    def receive(q, c):
+        @pl.when(q < me)
+        def _():
+            b = me - 1 - q
+            ag_copy(b, c, True).wait_recv()
+
+            @pl.when(me < last)
+            def _():
+                ag_copy(b, c, True).start()
+
+        @pl.when((q >= me) & (me > 0))
+        def _():
+            d = last - (q - me)
+            rs_copy(d, c, True).wait_recv()
+            part[d, chunk(c), :] = (
+                part[d, chunk(c), :].astype(jnp.float32)
+                + from_left[d, chunk(c), :].astype(jnp.float32)
+            ).astype(part.dtype)
+            rs_copy(d, c, True).start()
+
+        @pl.when(q < mirror)
+        def _():
+            b = me + 1 + q
+            ag_copy(b, c, False).wait_recv()
+
+            @pl.when(me > 0)
+            def _():
+                ag_copy(b, c, False).start()
+
+        @pl.when((q >= mirror) & (me < last))
+        def _():
+            d = q - mirror
+            rs_copy(d, c, False).wait_recv()
+            part[d, chunk(c), :] = (
+                part[d, chunk(c), :].astype(jnp.float32)
+                + from_right[d, chunk(c), :].astype(jnp.float32)
+            ).astype(part.dtype)
+            rs_copy(d, c, False).start()
+
+    @pl.loop(0, last)
+    def _(q):
+        @pl.loop(0, chunks)
+        def _(c):
+            receive(q, c)
+
+        @pl.when(q < me)
+        def _():
+            frozen(me - 1 - q, False)
+
+        @pl.when(q < mirror)
+        def _():
+            frozen(me + 1 + q, False)
+
+    for step in range(1, n):
+        source = lax.rem(me + step, n)
+        small_copy(source, source).wait_recv()
+    total = small[0].astype(jnp.float32)
+    for b in range(1, n):
+        total = total + small[b].astype(jnp.float32)
+    low = jnp.where(diagonal, jnp.concatenate([total[:rank]] * slots, axis=0), 0.0)
+    back = jnp.where(diagonal, jnp.concatenate([total[rank:]] * slots, axis=0), 0.0)
+    lowt[...] = low.astype(lowt.dtype)
+    backt[...] = back.astype(backt.dtype)
+    gup_ref[...] = (
+        adapter_scale
+        * jnp.dot(lowt[...], full[me], preferred_element_type=jnp.float32)
+    ).astype(gup_ref.dtype)
+
+    @pl.loop(0, depth // width)
+    def _(j):
+        gdown_ref[:, columns(j)] = jnp.dot(
+            backt[...], x_ref[:, columns(j)], preferred_element_type=jnp.float32
+        ).astype(gdown_ref.dtype)
+        gin_ref[:, columns(j)] = (
+            alive_ref[...]
+            * (
+                acc[:, columns(j)]
+                + lax.dot_general(
+                    backt[...], down_ref[:, columns(j)], TN, preferred_element_type=jnp.float32
+                )
+            )
+        ).astype(gin_ref.dtype)
+
+    acc[:, :width] = adapter_scale * lax.dot_general(
+        lowt[...], up_ref[...], TN, preferred_element_type=jnp.float32
+    )
+
+    def rs_finish(c, to_right):
+        rs_copy(me, c, to_right).wait_recv()
+        arrived = from_left if to_right else from_right
+        acc[chunk(c), :width] += arrived[me, chunk(c), :].astype(jnp.float32)
+
+    @pl.loop(0, chunks)
+    def _(c):
+        acc[chunk(c), :width] += part[me, chunk(c), :].astype(jnp.float32)
+
+        @pl.when(me > 0)
+        def _():
+            rs_finish(c, True)
+
+        @pl.when(me < last)
+        def _():
+            rs_finish(c, False)
+
+        kv_ref[chunk(c), :] = (alive_ref[chunk(c), :] * acc[chunk(c), :width]).astype(kv_ref.dtype)
+
+    def drain(b, c):
+        @pl.when((b <= me) & (me < last))
+        def _():
+            ag_copy(b, c, True).wait_send()
+
+        @pl.when((b >= me) & (me > 0))
+        def _():
+            ag_copy(b, c, False).wait_send()
+
+        @pl.when(b > me)
+        def _():
+            rs_copy(b, c, True).wait_send()
+
+        @pl.when(b < me)
+        def _():
+            rs_copy(b, c, False).wait_send()
+
+    for step in range(1, n):
+        small_copy(lax.rem(me + step, n), me).wait_send()
+
+    @pl.loop(0, n)
+    def _(b):
+        @pl.loop(0, chunks)
+        def _(c):
+            drain(b, c)
+
+
+def line_call(n, slots, x, w, cot, alive, down, up):
+    rows, depth = x.shape
+    width = cot.shape[1]
+    panel = down.shape[0]
+    rank = panel // slots
+    bf16 = jnp.bfloat16
+    vmem = pl.BlockSpec(memory_space=pltpu.VMEM)
+    hbm = pl.BlockSpec(memory_space=pl.ANY)
+    dma = pltpu.SemaphoreType.DMA((n, CHUNKS))
+    return pl.pallas_call(
+        functools.partial(line_kernel, n, CHUNKS, slots),
+        out_shape=(
+            jax.ShapeDtypeStruct((rows, width), bf16),
+            jax.ShapeDtypeStruct((rows, depth), bf16),
+            jax.ShapeDtypeStruct((panel, depth), bf16),
+            jax.ShapeDtypeStruct((panel, width), bf16),
+        ),
+        in_specs=[hbm, hbm, vmem, vmem, vmem, vmem],
+        out_specs=(vmem, vmem, vmem, vmem),
+        scratch_shapes=[
+            pltpu.VMEM((rows, depth), bf16),
+            pltpu.VMEM(w.shape, bf16),
+            pltpu.VMEM((n, rows, width), bf16),
+            pltpu.VMEM((n, rows, width), bf16),
+            pltpu.VMEM((n, rows, width), bf16),
+            pltpu.VMEM((n, rows, width), bf16),
+            pltpu.VMEM((rows, depth), jnp.float32),
+            pltpu.VMEM((n, 2 * rank, rows), bf16),
+            pltpu.VMEM((panel, rows), bf16),
+            pltpu.VMEM((panel, rows), bf16),
+            pltpu.SemaphoreType.DMA((2,)),
+            dma, dma, dma, dma, dma, dma, dma,
+            pltpu.SemaphoreType.DMA((n,)),
+            pltpu.SemaphoreType.DMA((n,)),
+        ],
+        compiler_params=pltpu.CompilerParams(
+            collective_id=0, has_side_effects=True, vmem_limit_bytes=56 << 20
+        ),
+        cost_estimate=pl.CostEstimate(
+            flops=4 * rows * depth * n * width, bytes_accessed=30_000_000, transcendentals=0
+        ),
+    )(x, w, cot, alive, down, up)
 
 
 def shards(
@@ -50,6 +373,58 @@
         & (mine_rank[:, None] == cap_ids[None, :])[:, None, :]
     ).astype(jnp.float32)
     live_sequence_mask = (slot_ids < group_live_counts[0]).astype(jnp.bfloat16)[:, None, None]
+    rank = adapter_down_weight.shape[1]
+    tensor_total = lax.axis_size("tensor")
+    rows = slot_count * seq_length
+    if (
+        tensor_total > 1
+        and output_portion % 128 == 0
+        and dim_shard % output_portion == 0
+        and rows % (16 * CHUNKS) == 0
+        and full_out * dim_shard <= 1 << 22
+    ):
+        exchange = functools.partial(
+            lax.all_to_all, axis_name="dp", split_axis=0, concat_axis=0, tiled=True
+        )
+        keep = selection.reshape(group_total * capacity, holder_count).astype(jnp.bfloat16)
+        pick = pick_table.reshape(slot_count, group_total * capacity).astype(jnp.bfloat16)
+
+        def bring(store):
+            flat = store.reshape(holder_count, -1)
+            chosen = jnp.dot(keep, flat, preferred_element_type=jnp.float32).astype(jnp.bfloat16)
+            came = exchange(chosen.reshape(group_total, capacity, -1)).reshape(
+                group_total * capacity, -1
+            )
+            mine = jnp.dot(pick, came, preferred_element_type=jnp.float32).astype(jnp.bfloat16)
+            return mine.reshape(slot_count * rank, -1)
+
+        def deliver(contribution):
+            flat = contribution.reshape(slot_count, -1)
+            sent = jnp.dot(pick.T, flat, preferred_element_type=jnp.float32).astype(jnp.bfloat16)
+            came = exchange(sent.reshape(group_total, capacity, -1)).reshape(
+                group_total * capacity, -1
+            )
+            stored = jnp.dot(keep.T, came, preferred_element_type=jnp.float32)
+            return stored.reshape(holder_count, rank, -1)
+
+        alive = (slot_ids < group_live_counts[0]).astype(jnp.float32)
+        alive = jnp.broadcast_to(alive[:, None], (slot_count, seq_length)).reshape(rows, 1)
+        key_value, grad_in, down_part, up_part = line_call(
+            tensor_total,
+            slot_count,
+            activations.reshape(rows, dim_shard),
+            frozen_weight,
+            cotangent.reshape(rows, output_portion),
+            alive,
+            bring(adapter_down_weight),
+            bring(adapter_up_weight),
+        )
+        return (
+            key_value.reshape(slot_count, seq_length, output_portion),
+            grad_in.reshape(slot_count, seq_length, dim_shard),
+            deliver(down_part),
+            deliver(up_part),
+        )
     every_down, every_up = (
         lax.all_gather(adapter_down_weight, "dp", axis=0, tiled=True),
         lax.all_gather(adapter_up_weight, "dp", axis=0, tiled=True),

time: 343 us -> 159 us (0.46)
  waiting for transfers between devices: 230 us -> 17.8 us
  Pallas kernels: 0 us -> 98.7 us
  matrix products: 53.3 us -> 3.4 us
  blocking collectives: 21.7 us -> 0 us
  between operations: 14.6 us -> 1.48 us
  starting transfers between devices: 6.96 us -> 14.7 us
  local copies, waits for them, and re-layouts: 14.4 us -> 21.3 us
    all_gather x3 -> x0, waiting for transfers between devices: 127 us -> none  [the longest x1 76.2 us: shards(): masked_full = lax.all_gather(masked, 'tensor', axis=2, tiled=True)]
    psum x1 -> x0, waiting for transfers between devices: 103 us -> none  [shards(): lax.psum(partial_value.astype(jnp.bfloat16), 'tensor').astype(jnp.float32)]
    pallas_call x0 -> x1, Pallas kernels: none -> 98.7 us  [line_call(): pl.pallas_call(functools.partial(line_kernel, n, CHUNKS, slots), out_shap...]
    dot_general x14 -> x8, matrix products: 53.1 us -> 3.2 us  [the longest x2 1.13 us: bring(): jnp.dot(pick, came, preferred_element_type=jnp.float32).astype(jnp.bfloat16)]
    psum x1 -> x0, blocking collectives: 21.7 us -> none  [shards(): lax.psum(jnp.einsum('cfy,cjy->cfj', activations, down_weight_slice, prefe...]
    all_to_all x2 -> x4, waiting for transfers between devices: 0.01 us -> 17.8 us  [the longest x2 9.83 us: deliver(): exchange(sent.reshape(group_total, capacity, -1))]
    reshape x0 -> x11, local copies, waits for them, and re-layouts: none -> 9.05 us  [the longest x2 2.25 us: deliver(): flat = contribution.reshape(slot_count, -1)]
    all_to_all x2 -> x4, starting transfers between devices: 6.8 us -> 14.7 us  [the longest x2 7.68 us: bring(): exchange(chosen.reshape(group_total, capacity, -1))]
  transfers between devices with their start and end apart: 6 -> 4, of which waited for: 4 -> 4; matrix products, arithmetic and copies ran while one was open for 18% -> 5% of each run, Pallas kernels for 0% -> 0%
where the time goes in v1:
time: 159 us; the launch traced here: 158 us
  Pallas kernels  98.7 us (62%)
  local copies, waits for them, and re-layouts  21.3 us (13%)
  waiting for transfers between devices  17.8 us (11%)
  starting transfers between devices  14.7 us (9%)
  matrix products  3.4 us (2%)
    pallas_call x1, Pallas kernels, line_call(): pl.pallas_call(functools.partial(line_kernel, n, CHUNKS, slots), out_shap...  98.7 us
    unnamed x14, local copies, waits for them, and re-layouts  11.4 us
    all_to_all x2, waiting for transfers between devices, deliver(): exchange(sent.reshape(group_total, capacity, -1))  9.83 us
    all_to_all x2, waiting for transfers between devices, bring(): exchange(chosen.reshape(group_total, capacity, -1))  7.97 us
    all_to_all x2, starting transfers between devices, bring(): exchange(chosen.reshape(group_total, capacity, -1))  7.68 us
    all_to_all x2, starting transfers between devices, deliver(): exchange(sent.reshape(group_total, capacity, -1))  6.98 us
  transfers between devices with their start and end apart: 4, of which 4 were waited for; matrix products, arithmetic and copies ran while one was open for 5% of the time, Pallas kernels for 0%

profile of v1, /device:TPU:0, one launch (start us, length us, event | category | flops | bytes accessed | tf_op | source)
XLA Modules:
  0.0 158.5 jit_solution(14131363147568857012)
XLA Ops:
  0.6 0.0 copy-start
  0.6 0.0 copy-start.2
  0.7 0.8 compare_select_fusion
  1.5 0.0 copy-done
  1.5 0.7 gather_fusion
  2.2 0.1 gather.6
  2.3 1.3 copy.32
  3.6 0.2 convert_reduce_fusion
  3.9 0.2 convolution_convert_fusion.4
  4.1 0.2 convolution_convert_fusion.3
  4.3 0.8 reshape.249
  5.0 4.2 %all-to-all-start.1 = ((bf16[4,2,8192]{2,1,0:T(2,128)(2,1)}), bf16[4,2,8192]{2,1,0:T(2,128)(2,1)S(1)}, u32[]{:S(2)}, u32[]{:S(2)}) async-start(bf16[4,2,8192]{2,1,0:T(2,128)(2,1)} %reshape.249), calls=%async_computation.1 | async-start | bytes 262144 | tf_op jit(solution)/shard_map/all_to_all | solution.py:395
  9.2 0.0 copy-done.2
  9.3 1.2 copy.31
  10.4 0.4 convolution_convert_fusion.1
  10.8 1.1 reshape.246
  12.6 0.1 broadcast_in_dim.4
  12.7 1.0 reshape.271.alive_ref
  13.7 0.2 all-to-all-done.1
  13.9 3.5 %all-to-all-start = ((bf16[4,2,32768]{2,1,0:T(2,128)(2,1)}), bf16[4,2,32768]{2,1,0:T(2,128)(2,1)S(1)}, u32[]{:S(2)}, u32[]{:S(2)}) async-start(bf16[4,2,32768]{2,1,0:T(2,128)(2,1)} %reshape.246), calls=%async_computation | async-start | bytes 1048576 | tf_op jit(solution)/shard_map/all_to_all | solution.py:395
  17.4 0.3 fusion.1
  17.7 0.7 reshape.250.up_ref
  18.4 7.8 %all-to-all-done = bf16[4,2,32768]{2,1,0:T(2,128)(2,1)S(1)} async-done(((bf16[4,2,32768]{2,1,0:T(2,128)(2,1)}), bf16[4,2,32768]{2,1,0:T(2,128)(2,1)S(1)}, u32[]{:S(2)}, u32[]{:S(2)}) %all-to-all-start) | async-done | bytes 524320 | tf_op jit(solution)/shard_map/all_to_all | solution.py:395
  26.1 0.8 fusion
  27.0 1.0 reshape.247.down_ref
  28.0 98.7 %shard_map.111 = (bf16[960,512]{1,0:T(8,128)(2,1)}, bf16[960,2048]{1,0:T(8,128)(2,1)}, bf16[128,2048]{1,0:T(8,128)(2,1)}, bf16[128,512]{1,0:T(8,128)(2,1)}) custom-call(bf16[960,2048]{1,0:T(8,128)(2,1)} %bitcast.60, bf16[2048,2048]{1,0:T(8,128)(2,1)} %w_hbm.1, bf16[960,512]{1,0:T(8,128)(2,1)} %bitcast.61, f32[960,1]{1,0:T(8,128)} %reshape.271.alive_ref, ...), custom_call_target="tpu_custom_call" | custom-call | flops 16106127360 | bytes 30000000 | tf_op jit(solution)/shard_map/pallas_call | solution.py:300
  126.8 1.3 reshape.253
  128.1 1.0 reshape.256
  129.0 0.2 convolution_convert_fusion.2
  129.2 0.8 reshape.257
  130.0 3.3 %all-to-all-start.3 = ((bf16[4,2,8192]{2,1,0:T(2,128)(2,1)}), bf16[4,2,8192]{2,1,0:T(2,128)(2,1)S(1)}, u32[]{:S(2)}, u32[]{:S(2)}) async-start(bf16[4,2,8192]{2,1,0:T(2,128)(2,1)} %reshape.257), calls=%async_computation.3 | async-start | bytes 262144 | tf_op jit(solution)/shard_map/all_to_all | solution.py:404
  133.3 0.3 convolution_convert_fusion
  133.6 1.1 reshape.254
  134.7 3.2 %all-to-all-done.3 = bf16[4,2,8192]{2,1,0:T(2,128)(2,1)S(1)} async-done(((bf16[4,2,8192]{2,1,0:T(2,128)(2,1)}), bf16[4,2,8192]{2,1,0:T(2,128)(2,1)S(1)}, u32[]{:S(2)}, u32[]{:S(2)}) %all-to-all-start.3) | async-done | bytes 131104 | tf_op jit(solution)/shard_map/all_to_all | solution.py:404
  137.9 3.7 %all-to-all-start.2 = ((bf16[4,2,32768]{2,1,0:T(2,128)(2,1)}), bf16[4,2,32768]{2,1,0:T(2,128)(2,1)S(1)}, u32[]{:S(2)}, u32[]{:S(2)}) async-start(bf16[4,2,32768]{2,1,0:T(2,128)(2,1)} %reshape.254), calls=%async_computation.2 | async-start | bytes 1048576 | tf_op jit(solution)/shard_map/all_to_all | solution.py:404
  141.6 0.1 reshape.258
  141.6 0.3 fusion.11
  142.0 1.6 copy.30
  143.5 6.7 %all-to-all-done.2 = bf16[4,2,32768]{2,1,0:T(2,128)(2,1)S(1)} async-done(((bf16[4,2,32768]{2,1,0:T(2,128)(2,1)}), bf16[4,2,32768]{2,1,0:T(2,128)(2,1)S(1)}, u32[]{:S(2)}, u32[]{:S(2)}) %all-to-all-start.2) | async-done | bytes 524320 | tf_op jit(solution)/shard_map/all_to_all | solution.py:404
  150.2 0.2 reshape.255
  150.4 0.7 fusion.10
  151.1 0.0 copy-start.3
  151.2 0.0 copy-start.1
  151.2 4.4 %copy.29 = f32[32,16,2048]{2,1,0:T(8,128)} copy(f32[32,16,2048]{2,0,1:T(8,128)S(1)} %fusion.10) | data formatting | bytes 8388608
  155.6 0.0 copy-done.3
  155.6 0.9 copy.36
  156.6 0.0 copy-done.1
  156.6 1.9 %copy.37 = bf16[8,120,2048]{2,1,0:T(8,128)(2,1)} copy(bf16[8,120,2048]{2,1,0:T(8,128)(2,1)S(1)} %bitcast.47) | data formatting | bytes 7864320
  (9 shorter events, 0.1 us)
Async XLA Ops:
  0.6 0.9 copy-start
  0.6 8.6 %copy-start.2 = (bf16[32,16,2048]{2,1,0:T(8,128)(2,1)S(1)}, bf16[32,16,2048]{2,1,0:T(8,128)(2,1)}, u32[]{:S(2)}) copy-start(bf16[32,16,2048]{2,1,0:T(8,128)(2,1)} %param.11) | copy-start | bytes 6291460
  5.0 8.8 %all-to-all-start.1 = ((bf16[4,2,8192]{2,1,0:T(2,128)(2,1)}), bf16[4,2,8192]{2,1,0:T(2,128)(2,1)S(1)}, u32[]{:S(2)}, u32[]{:S(2)}) async-start(bf16[4,2,8192]{2,1,0:T(2,128)(2,1)} %reshape.249), calls=%async_computation.1 | async-start | bytes 262144 | tf_op jit(solution)/shard_map/all_to_all | solution.py:395
  13.9 12.3 %all-to-all-start = ((bf16[4,2,32768]{2,1,0:T(2,128)(2,1)}), bf16[4,2,32768]{2,1,0:T(2,128)(2,1)S(1)}, u32[]{:S(2)}, u32[]{:S(2)}) async-start(bf16[4,2,32768]{2,1,0:T(2,128)(2,1)} %reshape.246), calls=%async_computation | async-start | bytes 1048576 | tf_op jit(solution)/shard_map/all_to_all | solution.py:395
  130.0 7.9 %all-to-all-start.3 = ((bf16[4,2,8192]{2,1,0:T(2,128)(2,1)}), bf16[4,2,8192]{2,1,0:T(2,128)(2,1)S(1)}, u32[]{:S(2)}, u32[]{:S(2)}) async-start(bf16[4,2,8192]{2,1,0:T(2,128)(2,1)} %reshape.257), calls=%async_computation.3 | async-start | bytes 262144 | tf_op jit(solution)/shard_map/all_to_all | solution.py:404
  137.9 12.3 %all-to-all-start.2 = ((bf16[4,2,32768]{2,1,0:T(2,128)(2,1)}), bf16[4,2,32768]{2,1,0:T(2,128)(2,1)S(1)}, u32[]{:S(2)}, u32[]{:S(2)}) async-start(bf16[4,2,32768]{2,1,0:T(2,128)(2,1)} %reshape.254), calls=%async_computation.2 | async-start | bytes 1048576 | tf_op jit(solution)/shard_map/all_to_all | solution.py:404
  151.1 4.5 %copy-start.3 = (bf16[960,512]{1,0:T(8,128)(2,1)S(1)}, bf16[960,512]{1,0:T(8,128)(2,1)}, u32[]{:S(2)}) copy-start(bf16[960,512]{1,0:T(8,128)(2,1)} %get-tuple-element.8) | copy-start | bytes 2949124
  151.2 5.4 %copy-start.1 = (bf16[960,2048]{1,0:T(8,128)(2,1)S(1)}, bf16[960,2048]{1,0:T(8,128)(2,1)}, u32[]{:S(2)}) copy-start(bf16[960,2048]{1,0:T(8,128)(2,1)} %get-tuple-element.9) | copy-start | bytes 11796484

commit v2 on v1

--- a/solution.py
+++ b/solution.py
@@ -20,9 +20,10 @@
 
 
 def line_kernel(
-    n, chunks, slots,
-    x_hbm, w_hbm, cot_ref, alive_ref, down_ref, up_ref,
-    kv_ref, gin_ref, gdown_ref, gup_ref,
+    n, groups, chunks, slots,
+    x_hbm, w_hbm, cot_ref, alive_ref, store_down, store_up, keep_ref, pick_ref,
+    kv_ref, gin_hbm, gdown_ref, gup_ref,
+    panels, asked, came, given, landed, dp_send, dp_recv,
     x_ref, w_ref, full, part, from_left, from_right, acc, small, lowt, backt,
     load_sem, ag_recv, ag_right, ag_left, rs_recv_r, rs_recv_l, rs_send_r, rs_send_l,
     small_send, small_recv,
@@ -72,6 +73,25 @@
             device_id_type=MESH,
         )
 
+    group = lax.axis_index("dp")
+    share = asked.shape[1]
+    parts = depth // width
+    down_ref = panels.at[:, pl.ds(0, depth)]
+    up_ref = panels.at[:, pl.ds(depth, width)]
+
+    def dp_copy(step, way, receiving):
+        peer = lax.rem(group + step, groups)
+        source, target = ((asked, came), (given, landed))[way]
+        slot = peer if receiving else group
+        return pltpu.make_async_remote_copy(
+            src_ref=source.at[peer],
+            dst_ref=target.at[slot],
+            send_sem=dp_send.at[way, peer],
+            recv_sem=dp_recv.at[way, slot],
+            device_id={"dp": peer},
+            device_id_type=MESH,
+        )
+
     load_x = pltpu.make_async_copy(x_hbm, x_ref, load_sem.at[0])
     load_w = pltpu.make_async_copy(w_hbm, w_ref, load_sem.at[1])
     load_x.start()
@@ -81,8 +101,12 @@
         pl.semaphore_signal(
             barrier, inc=1, device_id={"tensor": lax.rem(me + step, n)}, device_id_type=MESH
         )
+    for step in range(1, groups):
+        pl.semaphore_signal(
+            barrier, inc=1, device_id={"dp": lax.rem(group + step, groups)}, device_id_type=MESH
+        )
     full[me] = (cot_ref[...].astype(jnp.float32) * alive_ref[...]).astype(full.dtype)
-    pl.semaphore_wait(barrier, n - 1)
+    pl.semaphore_wait(barrier, n + groups - 2)
 
     @pl.loop(0, chunks)
     def _(c):
@@ -93,6 +117,20 @@
         @pl.when(me > 0)
         def _():
             ag_copy(me, c, False).start()
+
+    for j in range(parts + 1):
+        if j < parts:
+            store = store_down[:, j * width : (j + 1) * width]
+        else:
+            store = store_up[...]
+        chosen = jnp.dot(
+            keep_ref[...], store, preferred_element_type=jnp.float32
+        ).astype(asked.dtype)
+        for e in range(groups):
+            asked[e, :, j * width : (j + 1) * width] = chosen[e * share : (e + 1) * share]
+    for step in range(1, groups):
+        dp_copy(step, 0, False).start()
+    came[group] = asked[group]
 
     shape = (slots * rank, rows)
     slot_of_row = lax.broadcasted_iota(jnp.int32, shape, 0) // rank
@@ -106,17 +144,7 @@
             total = total + wide[s * rank : (s + 1) * rank]
         return total
 
-    back_part = compact(
-        lax.dot_general(up_ref[...], full[me], NT, preferred_element_type=jnp.float32)
-    )
-    small[me, rank:, :] = (adapter_scale * back_part).astype(small.dtype)
     load_x.wait()
-    low_part = compact(
-        lax.dot_general(down_ref[...], x_ref[...], NT, preferred_element_type=jnp.float32)
-    )
-    small[me, :rank, :] = low_part.astype(small.dtype)
-    for step in range(1, n):
-        small_copy(lax.rem(me + step, n), me).start()
     load_w.wait()
 
     @pl.loop(0, n)
@@ -136,6 +164,24 @@
             @pl.when((me == last) & (d < last))
             def _():
                 rs_copy(d, c, False).start()
+
+    for step in range(1, groups):
+        dp_copy(step, 0, True).wait_recv()
+    for j in range(parts + 1):
+        block = came[:, :, j * width : (j + 1) * width].reshape(groups * share, width)
+        panels[:, j * width : (j + 1) * width] = jnp.dot(
+            pick_ref[...], block, preferred_element_type=jnp.float32
+        ).astype(panels.dtype)
+    back_part = compact(
+        lax.dot_general(up_ref[...], full[me], NT, preferred_element_type=jnp.float32)
+    )
+    small[me, rank:, :] = (adapter_scale * back_part).astype(small.dtype)
+    low_part = compact(
+        lax.dot_general(down_ref[...], x_ref[...], NT, preferred_element_type=jnp.float32)
+    )
+    small[me, :rank, :] = low_part.astype(small.dtype)
+    for step in range(1, n):
+        small_copy(lax.rem(me + step, n), me).start()
 
     def frozen(b, first):
         @pl.loop(0, chunks)
@@ -194,8 +240,7 @@
             ).astype(part.dtype)
             rs_copy(d, c, False).start()
 
-    @pl.loop(0, last)
-    def _(q):
+    def round_of(q):
         @pl.loop(0, chunks)
         def _(c):
             receive(q, c)
@@ -207,6 +252,10 @@
         @pl.when(q < mirror)
         def _():
             frozen(me + 1 + q, False)
+
+    @pl.loop(0, last - 1)
+    def _(q):
+        round_of(q)
 
     for step in range(1, n):
         source = lax.rem(me + step, n)
@@ -218,25 +267,53 @@
     back = jnp.where(diagonal, jnp.concatenate([total[rank:]] * slots, axis=0), 0.0)
     lowt[...] = low.astype(lowt.dtype)
     backt[...] = back.astype(backt.dtype)
-    gup_ref[...] = (
-        adapter_scale
-        * jnp.dot(lowt[...], full[me], preferred_element_type=jnp.float32)
-    ).astype(gup_ref.dtype)
-
-    @pl.loop(0, depth // width)
+    for j in range(parts + 1):
+        if j < parts:
+            block = jnp.dot(
+                backt[...],
+                x_ref[:, j * width : (j + 1) * width],
+                preferred_element_type=jnp.float32,
+            )
+        else:
+            block = adapter_scale * jnp.dot(
+                lowt[...], full[me], preferred_element_type=jnp.float32
+            )
+        block = lax.dot_general(
+            pick_ref[...], block.astype(given.dtype), TN, preferred_element_type=jnp.float32
+        ).astype(given.dtype)
+        for e in range(groups):
+            given[e, :, j * width : (j + 1) * width] = block[e * share : (e + 1) * share]
+    for step in range(1, groups):
+        dp_copy(step, 1, False).start()
+    landed[group] = given[group]
+
+    round_of(last - 1)
+
+    @pl.loop(0, parts)
     def _(j):
-        gdown_ref[:, columns(j)] = jnp.dot(
-            backt[...], x_ref[:, columns(j)], preferred_element_type=jnp.float32
-        ).astype(gdown_ref.dtype)
-        gin_ref[:, columns(j)] = (
+        x_ref[:, columns(j)] = (
             alive_ref[...]
             * (
                 acc[:, columns(j)]
                 + lax.dot_general(
-                    backt[...], down_ref[:, columns(j)], TN, preferred_element_type=jnp.float32
+                    backt[...], panels[:, columns(j)], TN, preferred_element_type=jnp.float32
                 )
             )
-        ).astype(gin_ref.dtype)
+        ).astype(x_ref.dtype)
+
+    store_x = pltpu.make_async_copy(x_ref, gin_hbm, load_sem.at[2])
+    store_x.start()
+    for step in range(1, groups):
+        dp_copy(step, 1, True).wait_recv()
+    for j in range(parts + 1):
+        block = landed[:, :, j * width : (j + 1) * width].reshape(groups * share, width)
+        block = lax.dot_general(
+            keep_ref[...], block, TN, preferred_element_type=jnp.float32
+        )
+        if j < parts:
+            gdown_ref[:, j * width : (j + 1) * width] = block
+        else:
+            gup_ref[...] = block
 
     acc[:, :width] = adapter_scale * lax.dot_general(
         lowt[...], up_ref[...], TN, preferred_element_type=jnp.float32
@@ -280,6 +357,10 @@
 
     for step in range(1, n):
         small_copy(lax.rem(me + step, n), me).wait_send()
+    for step in range(1, groups):
+        dp_copy(step, 0, False).wait_send()
+        dp_copy(step, 1, False).wait_send()
+    store_x.wait()
 
     @pl.loop(0, n)
     def _(b):
@@ -288,26 +369,35 @@
             drain(b, c)
 
 
-def line_call(n, slots, x, w, cot, alive, down, up):
+def line_call(n, groups, slots, x, w, cot, alive, down, up, keep, pick):
     rows, depth = x.shape
     width = cot.shape[1]
-    panel = down.shape[0]
+    held = down.shape[0]
+    panel = pick.shape[0]
     rank = panel // slots
+    share = keep.shape[0] // groups
     bf16 = jnp.bfloat16
     vmem = pl.BlockSpec(memory_space=pltpu.VMEM)
     hbm = pl.BlockSpec(memory_space=pl.ANY)
     dma = pltpu.SemaphoreType.DMA((n, CHUNKS))
     return pl.pallas_call(
-        functools.partial(line_kernel, n, CHUNKS, slots),
+        functools.partial(line_kernel, n, groups, CHUNKS, slots),
         out_shape=(
             jax.ShapeDtypeStruct((rows, width), bf16),
             jax.ShapeDtypeStruct((rows, depth), bf16),
-            jax.ShapeDtypeStruct((panel, depth), bf16),
-            jax.ShapeDtypeStruct((panel, width), bf16),
+            jax.ShapeDtypeStruct((held, depth), jnp.float32),
+            jax.ShapeDtypeStruct((held, width), jnp.float32),
         ),
-        in_specs=[hbm, hbm, vmem, vmem, vmem, vmem],
-        out_specs=(vmem, vmem, vmem, vmem),
+        in_specs=[hbm, hbm, vmem, vmem, vmem, vmem, vmem, vmem],
+        out_specs=(vmem, hbm, vmem, vmem),
         scratch_shapes=[
+            pltpu.VMEM((panel, depth + width), bf16),
+            pltpu.VMEM((groups, share, depth + width), bf16),
+            pltpu.VMEM((groups, share, depth + width), bf16),
+            pltpu.VMEM((groups, share, depth + width), bf16),
+            pltpu.VMEM((groups, share, depth + width), bf16),
+            pltpu.SemaphoreType.DMA((2, groups)),
+            pltpu.SemaphoreType.DMA((2, groups)),
             pltpu.VMEM((rows, depth), bf16),
             pltpu.VMEM(w.shape, bf16),
             pltpu.VMEM((n, rows, width), bf16),
@@ -318,18 +408,18 @@
             pltpu.VMEM((n, 2 * rank, rows), bf16),
             pltpu.VMEM((panel, rows), bf16),
             pltpu.VMEM((panel, rows), bf16),
-            pltpu.SemaphoreType.DMA((2,)),
+            pltpu.SemaphoreType.DMA((3,)),
             dma, dma, dma, dma, dma, dma, dma,
             pltpu.SemaphoreType.DMA((n,)),
             pltpu.SemaphoreType.DMA((n,)),
         ],
         compiler_params=pltpu.CompilerParams(
-            collective_id=0, has_side_effects=True, vmem_limit_bytes=56 << 20
+            collective_id=0, has_side_effects=True, vmem_limit_bytes=60 << 20
         ),
         cost_estimate=pl.CostEstimate(
             flops=4 * rows * depth * n * width, bytes_accessed=30_000_000, transcendentals=0
         ),
-    )(x, w, cot, alive, down, up)
+    )(x, w, cot, alive, down, up, keep, pick)
 
 
 def shards(
@@ -381,49 +471,39 @@
         and output_portion % 128 == 0
         and dim_shard % output_portion == 0
         and rows % (16 * CHUNKS) == 0
+        and rank % 16 == 0
+        and group_total > 1
         and full_out * dim_shard <= 1 << 22
     ):
-        exchange = functools.partial(
-            lax.all_to_all, axis_name="dp", split_axis=0, concat_axis=0, tiled=True
-        )
         keep = selection.reshape(group_total * capacity, holder_count).astype(jnp.bfloat16)
         pick = pick_table.reshape(slot_count, group_total * capacity).astype(jnp.bfloat16)
 
-        def bring(store):
-            flat = store.reshape(holder_count, -1)
-            chosen = jnp.dot(keep, flat, preferred_element_type=jnp.float32).astype(jnp.bfloat16)
-            came = exchange(chosen.reshape(group_total, capacity, -1)).reshape(
-                group_total * capacity, -1
-            )
-            mine = jnp.dot(pick, came, preferred_element_type=jnp.float32).astype(jnp.bfloat16)
-            return mine.reshape(slot_count * rank, -1)
-
-        def deliver(contribution):
-            flat = contribution.reshape(slot_count, -1)
-            sent = jnp.dot(pick.T, flat, preferred_element_type=jnp.float32).astype(jnp.bfloat16)
-            came = exchange(sent.reshape(group_total, capacity, -1)).reshape(
-                group_total * capacity, -1
-            )
-            stored = jnp.dot(keep.T, came, preferred_element_type=jnp.float32)
-            return stored.reshape(holder_count, rank, -1)
+        def widen(table):
+            down, across = table.shape
+            unit = jnp.eye(rank, dtype=table.dtype)
+            wide = table[:, None, :, None] * unit[None, :, None, :]
+            return wide.reshape(down * rank, across * rank)
 
         alive = (slot_ids < group_live_counts[0]).astype(jnp.float32)
         alive = jnp.broadcast_to(alive[:, None], (slot_count, seq_length)).reshape(rows, 1)
         key_value, grad_in, down_part, up_part = line_call(
             tensor_total,
+            group_total,
             slot_count,
             activations.reshape(rows, dim_shard),
             frozen_weight,
             cotangent.reshape(rows, output_portion),
             alive,
-            bring(adapter_down_weight),
-            bring(adapter_up_weight),
+            adapter_down_weight.reshape(holder_count * rank, dim_shard),
+            adapter_up_weight.reshape(holder_count * rank, output_portion),
+            widen(keep),
+            widen(pick),
         )
         return (
             key_value.reshape(slot_count, seq_length, output_portion),
             grad_in.reshape(slot_count, seq_length, dim_shard),
-            deliver(down_part),
-            deliver(up_part),
+            down_part.reshape(holder_count, rank, dim_shard),
+            up_part.reshape(holder_count, rank, output_portion),
         )
     every_down, every_up = (
         lax.all_gather(adapter_down_weight, "dp", axis=0, tiled=True),

time: 159 us -> 143 us (0.90)
  Pallas kernels: 98.7 us -> 125 us
  waiting for transfers between devices: 17.8 us -> 0 us
  starting transfers between devices: 14.7 us -> 0 us
  local copies, waits for them, and re-layouts: 21.3 us -> 15.1 us
  matrix products: 3.4 us -> 0.19 us
    pallas_call x1, Pallas kernels: 98.7 us -> 125 us  [line_call(): pl.pallas_call(functools.partial(line_kernel, n, groups, CHUNKS, slots),...]
    all_to_all x4 -> x0, waiting for transfers between devices: 17.8 us -> none  [the longest x2 9.83 us: deliver(): exchange(sent.reshape(group_total, capacity, -1))]
    all_to_all x4 -> x0, starting transfers between devices: 14.7 us -> none  [the longest x2 7.68 us: bring(): exchange(chosen.reshape(group_total, capacity, -1))]
    reshape x10 -> x0, local copies, waits for them, and re-layouts: 8.08 us -> none  [the longest x2 2.25 us: deliver(): flat = contribution.reshape(slot_count, -1)]
    mul x0 -> x2, local copies, waits for them, and re-layouts: none -> 3.26 us  [widen(): wide = table[:, None, :, None] * unit[None, :, None, :]]
    dot_general x8 -> x0, matrix products: 3.2 us -> none  [the longest x2 1.13 us: bring(): jnp.dot(pick, came, preferred_element_type=jnp.float32).astype(jnp.bfloat16)]
    unnamed x14 -> x10, local copies, waits for them, and re-layouts: 11.4 us -> 9.94 us
  transfers between devices with their start and end apart: 4 -> 0, of which waited for: 4 -> 0; matrix products, arithmetic and copies ran while one was open for 5% -> 0% of each run, Pallas kernels for 0% -> 0%
where the time goes in v2:
time: 143 us
  Pallas kernels  125 us (87%)
  local copies, waits for them, and re-layouts  15.1 us (11%)
    pallas_call x1, Pallas kernels, line_call(): pl.pallas_call(functools.partial(line_kernel, n, groups, CHUNKS, slots),...  125 us
    unnamed x10, local copies, waits for them, and re-layouts  9.94 us
    mul x2, local copies, waits for them, and re-layouts, widen(): wide = table[:, None, :, None] * unit[None, :, None, :]  3.26 us

profile of v2, /device:TPU:0, one launch (start us, length us, event | category | flops | bytes accessed | tf_op | source)
XLA Modules:
  0.0 143.0 jit_solution(11953320152878474052)
XLA Ops:
  0.6 0.0 copy-start
  1.3 0.7 compare_select_fusion
  2.0 0.0 copy-done
  2.0 0.7 gather_fusion
  2.7 0.1 gather.6
  2.8 0.2 convert_reduce_fusion
  3.0 0.2 convolution_convert_fusion
  3.3 0.1 copy.15
  3.4 0.1 broadcast_in_dim.4
  3.4 0.1 broadcast_multiply_fusion.1
  3.5 0.8 mul.41.pick_ref
  4.3 1.0 reshape.246.alive_ref
  5.3 0.1 broadcast_multiply_fusion
  5.4 2.5 %mul.37.keep_ref = bf16[128,512]{1,0:T(8,128)(2,1)} reshape(bf16[8,16,32,16]{3,2,1,0:T(8,128)(2,1)S(1)} %broadcast_multiply_fusion) | data formatting | bytes 262144 | tf_op jit(solution)/shard_map/mul | solution.py:484
  7.9 125.1 %shard_map.111 = (bf16[960,512]{1,0:T(8,128)(2,1)}, bf16[960,2048]{1,0:T(8,128)(2,1)}, f32[512,2048]{1,0:T(8,128)}, f32[512,512]{1,0:T(8,128)}) custom-call(bf16[960,2048]{1,0:T(8,128)(2,1)} %bitcast.26, bf16[2048,2048]{1,0:T(8,128)(2,1)} %w_hbm.1, bf16[960,512]{1,0:T(8,128)(2,1)} %bitcast.28, f32[960,1]{1,0:T(8,128)} %reshape.246.alive_ref, ...), custom_call_target="tpu_custom_call" | custom-call | flops 16106127360 | bytes 30000000 | tf_op jit(solution)/shard_map/pallas_call | solution.py:383
  133.0 2.2 %copy.22 = bf16[8,120,512]{2,1,0:T(8,128)(2,1)} copy(bf16[8,120,512]{2,1,0:T(8,128)(2,1)} %bitcast.23) | data formatting | bytes 1966080
  135.2 0.0 copy-start.1
  135.2 4.7 %copy.23 = bf16[8,120,2048]{2,1,0:T(8,128)(2,1)} copy(bf16[8,120,2048]{2,1,0:T(8,128)(2,1)} %bitcast.21) | data formatting | bytes 7864320
  140.0 0.0 copy-done.1
  140.0 0.0 copy-start.2
  140.0 2.0 %copy.24 = f32[32,16,2048]{2,1,0:T(8,128)} copy(f32[32,16,2048]{2,1,0:T(8,128)S(1)} %bitcast.20) | data formatting | bytes 8388608
  142.0 0.0 copy-done.2
  142.0 1.0 copy.25
  (10 shorter events, 0.1 us)
Async XLA Ops:
  0.6 1.4 copy-start
  135.2 4.7 %copy-start.1 = (f32[512,2048]{1,0:T(8,128)S(1)}, f32[512,2048]{1,0:T(8,128)}, u32[]{:S(2)}) copy-start(f32[512,2048]{1,0:T(8,128)} %get-tuple-element.10) | copy-start | bytes 12582916
  140.0 2.0 %copy-start.2 = (f32[512,512]{1,0:T(8,128)S(1)}, f32[512,512]{1,0:T(8,128)}, u32[]{:S(2)}) copy-start(f32[512,512]{1,0:T(8,128)} %get-tuple-element.11) | copy-start | bytes 3145732

commit v3 on v2

--- a/solution.py
+++ b/solution.py
@@ -21,9 +21,9 @@
 
 def line_kernel(
     n, groups, chunks, slots,
-    x_hbm, w_hbm, cot_ref, alive_ref, store_down, store_up, keep_ref, pick_ref,
-    kv_ref, gin_hbm, gdown_ref, gup_ref,
-    panels, asked, came, given, landed, dp_send, dp_recv,
+    x_hbm, w_hbm, cot_ref, live_ref, store_down, store_up, keep_ref, pick_ref,
+    kv_ref, gin_hbm, back_ref, up_back_ref,
+    alive_ref, panels, asked, came, given, landed, dp_send, dp_recv,
     x_ref, w_ref, full, part, from_left, from_right, acc, small, lowt, backt,
     load_sem, ag_recv, ag_right, ag_left, rs_recv_r, rs_recv_l, rs_send_r, rs_send_l,
     small_send, small_recv,
@@ -105,19 +105,10 @@
         pl.semaphore_signal(
             barrier, inc=1, device_id={"dp": lax.rem(group + step, groups)}, device_id_type=MESH
         )
+    alive_ref[...] = jnp.concatenate(
+        [jnp.broadcast_to(live_ref[s : s + 1, :1], (length, 1)) for s in range(slots)], axis=0
+    )
     full[me] = (cot_ref[...].astype(jnp.float32) * alive_ref[...]).astype(full.dtype)
-    pl.semaphore_wait(barrier, n + groups - 2)
-
-    @pl.loop(0, chunks)
-    def _(c):
-        @pl.when(me < last)
-        def _():
-            ag_copy(me, c, True).start()
-
-        @pl.when(me > 0)
-        def _():
-            ag_copy(me, c, False).start()
-
     for j in range(parts + 1):
         if j < parts:
             store = store_down[:, j * width : (j + 1) * width]
@@ -128,9 +119,21 @@
         ).astype(asked.dtype)
         for e in range(groups):
             asked[e, :, j * width : (j + 1) * width] = chosen[e * share : (e + 1) * share]
+    pl.semaphore_wait(barrier, n + groups - 2)
     for step in range(1, groups):
         dp_copy(step, 0, False).start()
     came[group] = asked[group]
+
+
+    @pl.loop(0, chunks)
+    def _(c):
+        @pl.when(me < last)
+        def _():
+            ag_copy(me, c, True).start()
+
+        @pl.when(me > 0)
+        def _():
+            ag_copy(me, c, False).start()
 
     shape = (slots * rank, rows)
     slot_of_row = lax.broadcasted_iota(jnp.int32, shape, 0) // rank
@@ -199,8 +202,6 @@
                 else:
                     acc[chunk(c), columns(j)] += piece
 
-    frozen(me, True)
-
     def receive(q, c):
         @pl.when(q < me)
         def _():
@@ -240,11 +241,12 @@
             ).astype(part.dtype)
             rs_copy(d, c, False).start()
 
-    def round_of(q):
+    def arrivals(q):
         @pl.loop(0, chunks)
         def _(c):
             receive(q, c)
 
+    def products(q):
         @pl.when(q < me)
         def _():
             frozen(me - 1 - q, False)
@@ -253,9 +255,9 @@
         def _():
             frozen(me + 1 + q, False)
 
-    @pl.loop(0, last - 1)
-    def _(q):
-        round_of(q)
+    arrivals(0)
+    frozen(me, True)
+    products(0)
 
     for step in range(1, n):
         source = lax.rem(me + step, n)
@@ -287,7 +289,10 @@
         dp_copy(step, 1, False).start()
     landed[group] = given[group]
 
-    round_of(last - 1)
+    @pl.loop(1, last)
+    def _(q):
+        arrivals(q)
+        products(q)
 
     @pl.loop(0, parts)
     def _(j):
@@ -305,15 +310,8 @@
     store_x.start()
     for step in range(1, groups):
         dp_copy(step, 1, True).wait_recv()
-    for j in range(parts + 1):
-        block = landed[:, :, j * width : (j + 1) * width].reshape(groups * share, width)
-        block = lax.dot_general(
-            keep_ref[...], block, TN, preferred_element_type=jnp.float32
-        )
-        if j < parts:
-            gdown_ref[:, j * width : (j + 1) * width] = block
-        else:
-            gup_ref[...] = block
+    back_ref[...] = landed[:, :, :depth].reshape(back_ref.shape)
+    up_back_ref[...] = landed[:, :, depth:].reshape(up_back_ref.shape)
 
     acc[:, :width] = adapter_scale * lax.dot_general(
         lowt[...], up_ref[...], TN, preferred_element_type=jnp.float32
@@ -372,7 +370,6 @@
 def line_call(n, groups, slots, x, w, cot, alive, down, up, keep, pick):
     rows, depth = x.shape
     width = cot.shape[1]
-    held = down.shape[0]
     panel = pick.shape[0]
     rank = panel // slots
     share = keep.shape[0] // groups
@@ -385,12 +382,13 @@
         out_shape=(
             jax.ShapeDtypeStruct((rows, width), bf16),
             jax.ShapeDtypeStruct((rows, depth), bf16),
-            jax.ShapeDtypeStruct((held, depth), jnp.float32),
-            jax.ShapeDtypeStruct((held, width), jnp.float32),
+            jax.ShapeDtypeStruct((keep.shape[0], depth), bf16),
+            jax.ShapeDtypeStruct((keep.shape[0], width), bf16),
         ),
         in_specs=[hbm, hbm, vmem, vmem, vmem, vmem, vmem, vmem],
         out_specs=(vmem, hbm, vmem, vmem),
         scratch_shapes=[
+            pltpu.VMEM((rows, 1), jnp.float32),
             pltpu.VMEM((panel, depth + width), bf16),
             pltpu.VMEM((groups, share, depth + width), bf16),
             pltpu.VMEM((groups, share, depth + width), bf16),
@@ -480,12 +478,23 @@
 
         def widen(table):
             down, across = table.shape
-            unit = jnp.eye(rank, dtype=table.dtype)
-            wide = table[:, None, :, None] * unit[None, :, None, :]
-            return wide.reshape(down * rank, across * rank)
+            spot = jnp.arange(1, across + 1, dtype=jnp.float32)
+            hit = jnp.sum(table.astype(jnp.float32) * spot, axis=1).astype(jnp.int32) - 1
+            target = hit[:, None] * rank + jnp.arange(rank, dtype=jnp.int32)
+            target = jnp.where(hit[:, None] < 0, -1, target).reshape(down * rank)
+            spots = jnp.arange(across * rank, dtype=jnp.int32)
+            return (target[:, None] == spots[None, :]).astype(jnp.bfloat16)
+
+        keep_wide = widen(keep)
+
+        def stored(came):
+            rows_of = lax.dot_general(
+                keep_wide, came, (((0,), (0,)), ((), ())), preferred_element_type=jnp.float32
+            )
+            return rows_of.reshape(holder_count, rank, came.shape[1])
 
         alive = (slot_ids < group_live_counts[0]).astype(jnp.float32)
-        alive = jnp.broadcast_to(alive[:, None], (slot_count, seq_length)).reshape(rows, 1)
+        alive = jnp.broadcast_to(alive[:, None], (slot_count, 128))
         key_value, grad_in, down_part, up_part = line_call(
             tensor_total,
             group_total,
@@ -496,14 +505,14 @@
             alive,
             adapter_down_weight.reshape(holder_count * rank, dim_shard),
             adapter_up_weight.reshape(holder_count * rank, output_portion),
-            widen(keep),
+            keep_wide,
             widen(pick),
         )
         return (
             key_value.reshape(slot_count, seq_length, output_portion),
             grad_in.reshape(slot_count, seq_length, dim_shard),
-            down_part.reshape(holder_count, rank, dim_shard),
-            up_part.reshape(holder_count, rank, output_portion),
+            stored(down_part),
+            stored(up_part),
         )
     every_down, every_up = (
         lax.all_gather(adapter_down_weight, "dp", axis=0, tiled=True),

time: 143 us -> 159 us (1.11)
  Pallas kernels: 125 us -> 145 us
  local copies, waits for them, and re-layouts: 15.1 us -> 4.67 us
  matrix products: 0.19 us -> 5.69 us
    pallas_call x1, Pallas kernels: 125 us -> 145 us  [line_call(): pl.pallas_call(functools.partial(line_kernel, n, groups, CHUNKS, slots),...]
    unnamed x10, local copies, waits for them, and re-layouts: 9.94 us -> 2.89 us
    dot_general x0 -> x2, matrix products: none -> 5.41 us  [stored(): lax.dot_general(keep_wide, came, (((0,), (0,)), ((), ())), preferred_elem...]
    mul x2 -> x1, local copies, waits for them, and re-layouts: 3.26 us -> 0.09 us  [widen(): target = hit[:, None] * rank + jnp.arange(rank, dtype=jnp.int32)]
where the time goes in v3:
time: 159 us
  Pallas kernels  145 us (91%)
  matrix products  5.69 us (4%)
  local copies, waits for them, and re-layouts  4.67 us (3%)
  other arithmetic  2.69 us (2%)
    pallas_call x1, Pallas kernels, line_call(): pl.pallas_call(functools.partial(line_kernel, n, groups, CHUNKS, slots),...  145 us
    dot_general x2, matrix products, stored(): lax.dot_general(keep_wide, came, (((0,), (0,)), ((), ())), preferred_elem...  5.41 us

profile of v3, /device:TPU:0, one launch (start us, length us, event | category | flops | bytes accessed | tf_op | source)
XLA Modules:
  0.0 159.0 jit_solution(13275000059781430095)
XLA Ops:
  0.6 0.0 copy-start
  1.3 0.7 broadcast_in_dim.18.live_ref
  2.0 0.7 compare_select_fusion
  2.6 0.0 copy-done
  2.6 0.7 gather_fusion
  3.3 0.1 gather.6
  3.5 0.2 convert_reduce_fusion
  3.7 0.3 fusion.2
  4.0 0.1 mul.40
  4.1 0.1 lt.72
  4.2 0.1 add_select_fusion.1
  4.2 0.1 select_n.61
  4.3 0.8 fusion.5.keep_ref
  5.1 0.1 multiply_reduce_fusion
  5.2 0.1 add_select_fusion
  5.3 0.1 select_n.64
  5.4 0.7 fusion.8.pick_ref
  6.1 144.5 %shard_map.111 = (bf16[960,512]{1,0:T(8,128)(2,1)}, bf16[960,2048]{1,0:T(8,128)(2,1)}, bf16[128,2048]{1,0:T(8,128)(2,1)}, bf16[128,512]{1,0:T(8,128)(2,1)}) custom-call(bf16[960,2048]{1,0:T(8,128)(2,1)} %bitcast.20, bf16[2048,2048]{1,0:T(8,128)(2,1)} %w_hbm.1, bf16[960,512]{1,0:T(8,128)(2,1)} %bitcast.22, f32[8,128]{1,0:T(8,128)} %broadcast_in_dim.18.live_ref, ...), custom_call_target="tpu_custom_call" | custom-call | flops 16106127360 | bytes 30000000 | tf_op jit(solution)/shard_map/pallas_call | solution.py:380
  150.7 0.0 copy-start.3
  150.7 0.0 copy-start.2
  150.7 0.0 copy-start.1
  150.7 4.0 %fusion.4 = f32[512,2048]{1,0:T(8,128)} fusion(bf16[128,2048]{1,0:T(8,128)(2,1)} %get-tuple-element.10, s32[128]{0:T(128)S(1)} %select_n.61), kind=kOutput, calls=%fused_computation.7 | convolution fusion | flops 268500992 | bytes 4719104 | tf_op jit(solution)/shard_map/dot_general | solution.py:491
  154.7 0.0 copy-done.3
  154.7 1.4 fusion.3
  156.1 0.0 copy-done.2
  156.1 0.9 copy.15
  157.1 0.0 copy-done.1
  157.1 1.9 %copy.16 = bf16[8,120,2048]{2,1,0:T(8,128)(2,1)} copy(bf16[8,120,2048]{2,1,0:T(8,128)(2,1)S(1)} %bitcast.17) | data formatting | bytes 7864320
  (14 shorter events, 0.1 us)
Async XLA Ops:
  0.6 2.0 %copy-start = (s32[128]{0:T(128)S(1)}, s32[128]{0:T(128)}, u32[]{:S(2)}) copy-start(s32[128]{0:T(128)} %param.14) | copy-start | bytes 1540
  150.7 4.1 %copy-start.3 = (bf16[128,512]{1,0:T(8,128)(2,1)S(1)}, bf16[128,512]{1,0:T(8,128)(2,1)}, u32[]{:S(2)}) copy-start(bf16[128,512]{1,0:T(8,128)(2,1)} %get-tuple-element.11) | copy-start | bytes 393220
  150.7 5.4 %copy-start.2 = (bf16[960,512]{1,0:T(8,128)(2,1)S(1)}, bf16[960,512]{1,0:T(8,128)(2,1)}, u32[]{:S(2)}) copy-start(bf16[960,512]{1,0:T(8,128)(2,1)} %get-tuple-element.8) | copy-start | bytes 2949124
  150.7 6.4 %copy-start.1 = (bf16[960,2048]{1,0:T(8,128)(2,1)S(1)}, bf16[960,2048]{1,0:T(8,128)(2,1)}, u32[]{:S(2)}) copy-start(bf16[960,2048]{1,0:T(8,128)(2,1)} %get-tuple-element.9) | copy-start | bytes 11796484

commit v4 on v3

--- a/solution.py
+++ b/solution.py
@@ -125,16 +125,18 @@
     came[group] = asked[group]
 
 
-    @pl.loop(0, chunks)
-    def _(c):
-        @pl.when(me < last)
-        def _():
-            ag_copy(me, c, True).start()
-
-        @pl.when(me > 0)
-        def _():
-            ag_copy(me, c, False).start()
-
+    def offer(low_chunk, high_chunk):
+        @pl.loop(low_chunk, high_chunk)
+        def _(c):
+            @pl.when(me < last)
+            def _():
+                ag_copy(me, c, True).start()
+
+            @pl.when(me > 0)
+            def _():
+                ag_copy(me, c, False).start()
+
+    offer(0, chunks // 2)
     shape = (slots * rank, rows)
     slot_of_row = lax.broadcasted_iota(jnp.int32, shape, 0) // rank
     slot_of_column = lax.broadcasted_iota(jnp.int32, shape, 1) // length
@@ -146,27 +148,6 @@
         for s in range(1, slots):
             total = total + wide[s * rank : (s + 1) * rank]
         return total
-
-    load_x.wait()
-    load_w.wait()
-
-    @pl.loop(0, n)
-    def _(k):
-        d = jnp.where(me == 0, last - k, k)
-
-        @pl.loop(0, chunks)
-        def _(c):
-            part[d, chunk(c), :] = jnp.dot(
-                x_ref[chunk(c), :], w_ref[:, columns(d)], preferred_element_type=jnp.float32
-            ).astype(part.dtype)
-
-            @pl.when((me == 0) & (d > 0))
-            def _():
-                rs_copy(d, c, True).start()
-
-            @pl.when((me == last) & (d < last))
-            def _():
-                rs_copy(d, c, False).start()
 
     for step in range(1, groups):
         dp_copy(step, 0, True).wait_recv()
@@ -179,12 +160,34 @@
         lax.dot_general(up_ref[...], full[me], NT, preferred_element_type=jnp.float32)
     )
     small[me, rank:, :] = (adapter_scale * back_part).astype(small.dtype)
+    load_x.wait()
     low_part = compact(
         lax.dot_general(down_ref[...], x_ref[...], NT, preferred_element_type=jnp.float32)
     )
     small[me, :rank, :] = low_part.astype(small.dtype)
     for step in range(1, n):
         small_copy(lax.rem(me + step, n), me).start()
+
+    offer(chunks // 2, chunks)
+    load_w.wait()
+
+    @pl.loop(0, n)
+    def _(k):
+        d = jnp.where(me == 0, last - k, k)
+
+        @pl.loop(0, chunks)
+        def _(c):
+            part[d, chunk(c), :] = jnp.dot(
+                x_ref[chunk(c), :], w_ref[:, columns(d)], preferred_element_type=jnp.float32
+            ).astype(part.dtype)
+
+            @pl.when((me == 0) & (d > 0))
+            def _():
+                rs_copy(d, c, True).start()
+
+            @pl.when((me == last) & (d < last))
+            def _():
+                rs_copy(d, c, False).start()
 
     def frozen(b, first):
         @pl.loop(0, chunks)
@@ -258,6 +261,11 @@
     arrivals(0)
     frozen(me, True)
     products(0)
+
+    @pl.loop(1, last - 1)
+    def _(q):
+        arrivals(q)
+        products(q)
 
     for step in range(1, n):
         source = lax.rem(me + step, n)
@@ -289,7 +297,7 @@
         dp_copy(step, 1, False).start()
     landed[group] = given[group]
 
-    @pl.loop(1, last)
+    @pl.loop(max(last - 1, 1), last)
     def _(q):
         arrivals(q)
         products(q)
@@ -308,33 +316,33 @@
 
     store_x = pltpu.make_async_copy(x_ref, gin_hbm, load_sem.at[2])
     store_x.start()
+    acc[:, :width] = adapter_scale * lax.dot_general(
+        lowt[...], up_ref[...], TN, preferred_element_type=jnp.float32
+    )
+
+    def rs_finish(c, to_right):
+        rs_copy(me, c, to_right).wait_recv()
+        arrived = from_left if to_right else from_right
+        acc[chunk(c), :width] += arrived[me, chunk(c), :].astype(jnp.float32)
+
+    @pl.loop(0, chunks)
+    def _(c):
+        acc[chunk(c), :width] += part[me, chunk(c), :].astype(jnp.float32)
+
+        @pl.when(me > 0)
+        def _():
+            rs_finish(c, True)
+
+        @pl.when(me < last)
+        def _():
+            rs_finish(c, False)
+
+        kv_ref[chunk(c), :] = (alive_ref[chunk(c), :] * acc[chunk(c), :width]).astype(kv_ref.dtype)
+
     for step in range(1, groups):
         dp_copy(step, 1, True).wait_recv()
     back_ref[...] = landed[:, :, :depth].reshape(back_ref.shape)
     up_back_ref[...] = landed[:, :, depth:].reshape(up_back_ref.shape)
-
-    acc[:, :width] = adapter_scale * lax.dot_general(
-        lowt[...], up_ref[...], TN, preferred_element_type=jnp.float32
-    )
-
-    def rs_finish(c, to_right):
-        rs_copy(me, c, to_right).wait_recv()
-        arrived = from_left if to_right else from_right
-        acc[chunk(c), :width] += arrived[me, chunk(c), :].astype(jnp.float32)
-
-    @pl.loop(0, chunks)
-    def _(c):
-        acc[chunk(c), :width] += part[me, chunk(c), :].astype(jnp.float32)
-
-        @pl.when(me > 0)
-        def _():
-            rs_finish(c, True)
-
-        @pl.when(me < last)
-        def _():
-            rs_finish(c, False)
-
-        kv_ref[chunk(c), :] = (alive_ref[chunk(c), :] * acc[chunk(c), :width]).astype(kv_ref.dtype)
 
     def drain(b, c):
         @pl.when((b <= me) & (me < last))

time: 159 us -> 113 us (0.71)
  Pallas kernels: 145 us -> 98.8 us
    pallas_call x1, Pallas kernels: 145 us -> 98.8 us  [line_call(): pl.pallas_call(functools.partial(line_kernel, n, groups, CHUNKS, slots),...]
where the time goes in v4:
time: 113 us
  Pallas kernels  98.8 us (87%)
  matrix products  5.69 us (5%)
  local copies, waits for them, and re-layouts  4.67 us (4%)
  other arithmetic  2.69 us (2%)
  between operations  1.38 us (1%)
    pallas_call x1, Pallas kernels, line_call(): pl.pallas_call(functools.partial(line_kernel, n, groups, CHUNKS, slots),...  98.8 us
    dot_general x2, matrix products, stored(): lax.dot_general(keep_wide, came, (((0,), (0,)), ((), ())), preferred_elem...  5.42 us
    unnamed x10, local copies, waits for them, and re-layouts  2.89 us

profile of v4, /device:TPU:0, one launch (start us, length us, event | category | flops | bytes accessed | tf_op | source)
XLA Modules:
  0.0 113.2 jit_solution(5461109893121799332)
XLA Ops:
  0.6 0.0 copy-start
  1.3 0.7 broadcast_in_dim.18.live_ref
  2.0 0.7 compare_select_fusion
  2.6 0.0 copy-done
  2.6 0.7 gather_fusion
  3.3 0.1 gather.6
  3.5 0.2 convert_reduce_fusion
  3.7 0.3 fusion.2
  4.0 0.1 mul.40
  4.1 0.1 lt.72
  4.2 0.1 add_select_fusion.1
  4.2 0.1 select_n.61
  4.3 0.8 fusion.5.keep_ref
  5.1 0.1 multiply_reduce_fusion
  5.2 0.1 add_select_fusion
  5.3 0.1 select_n.64
  5.4 0.7 fusion.8.pick_ref
  6.1 98.8 %shard_map.111 = (bf16[960,512]{1,0:T(8,128)(2,1)}, bf16[960,2048]{1,0:T(8,128)(2,1)}, bf16[128,2048]{1,0:T(8,128)(2,1)}, bf16[128,512]{1,0:T(8,128)(2,1)}) custom-call(bf16[960,2048]{1,0:T(8,128)(2,1)} %bitcast.20, bf16[2048,2048]{1,0:T(8,128)(2,1)} %w_hbm.1, bf16[960,512]{1,0:T(8,128)(2,1)} %bitcast.22, f32[8,128]{1,0:T(8,128)} %broadcast_in_dim.18.live_ref, ...), custom_call_target="tpu_custom_call" | custom-call | flops 16106127360 | bytes 30000000 | tf_op jit(solution)/shard_map/pallas_call | solution.py:388
  104.9 0.0 copy-start.3
  104.9 0.0 copy-start.2
  104.9 0.0 copy-start.1
  104.9 4.0 %fusion.4 = f32[512,2048]{1,0:T(8,128)} fusion(bf16[128,2048]{1,0:T(8,128)(2,1)} %get-tuple-element.10, s32[128]{0:T(128)S(1)} %select_n.61), kind=kOutput, calls=%fused_computation.7 | convolution fusion | flops 268500992 | bytes 4719104 | tf_op jit(solution)/shard_map/dot_general | solution.py:499
  108.9 0.0 copy-done.3
  108.9 1.4 %fusion.3 = f32[512,512]{1,0:T(8,128)} fusion(bf16[128,512]{1,0:T(8,128)(2,1)S(1)} %copy-done.3, s32[128]{0:T(128)S(1)} %select_n.61), kind=kOutput, calls=%fused_computation.6 | convolution fusion | flops 67174400 | bytes 1180160 | tf_op jit(solution)/shard_map/dot_general | solution.py:499
  110.3 0.0 copy-done.2
  110.3 0.9 copy.15
  111.3 0.0 copy-done.1
  111.3 1.9 %copy.16 = bf16[8,120,2048]{2,1,0:T(8,128)(2,1)} copy(bf16[8,120,2048]{2,1,0:T(8,128)(2,1)S(1)} %bitcast.17) | data formatting | bytes 7864320
  (14 shorter events, 0.1 us)
Async XLA Ops:
  0.6 2.0 %copy-start = (s32[128]{0:T(128)S(1)}, s32[128]{0:T(128)}, u32[]{:S(2)}) copy-start(s32[128]{0:T(128)} %param.14) | copy-start | bytes 1540
  104.9 4.1 %copy-start.3 = (bf16[128,512]{1,0:T(8,128)(2,1)S(1)}, bf16[128,512]{1,0:T(8,128)(2,1)}, u32[]{:S(2)}) copy-start(bf16[128,512]{1,0:T(8,128)(2,1)} %get-tuple-element.11) | copy-start | bytes 393220
  104.9 5.4 %copy-start.2 = (bf16[960,512]{1,0:T(8,128)(2,1)S(1)}, bf16[960,512]{1,0:T(8,128)(2,1)}, u32[]{:S(2)}) copy-start(bf16[960,512]{1,0:T(8,128)(2,1)} %get-tuple-element.8) | copy-start | bytes 2949124
  104.9 6.4 %copy-start.1 = (bf16[960,2048]{1,0:T(8,128)(2,1)S(1)}, bf16[960,2048]{1,0:T(8,128)(2,1)}, u32[]{:S(2)}) copy-start(bf16[960,2048]{1,0:T(8,128)(2,1)} %get-tuple-element.9) | copy-start | bytes 11796484

commit v5 on v4

--- a/solution.py
+++ b/solution.py
@@ -13,7 +13,7 @@
 adapter_scale = 2.0
 
 
-CHUNKS = 4
+CHUNKS = 5
 MESH = pl.DeviceIdType.MESH
 NT = (((1,), (1,)), ((), ()))
 TN = (((0,), (0,)), ((), ()))

time: 113 us -> 117 us (1.035)
  Pallas kernels: 98.8 us -> 102 us
    pallas_call x1, Pallas kernels: 98.8 us -> 102 us  [line_call(): pl.pallas_call(functools.partial(line_kernel, n, groups, CHUNKS, slots),...]
where the time goes in v5:
time: 117 us; the launch traced here: 116 us
  Pallas kernels  102 us (87%)
  matrix products  5.69 us (5%)
  local copies, waits for them, and re-layouts  4.67 us (4%)
  other arithmetic  2.69 us (2%)
  between operations  1.38 us (1%)
    pallas_call x1, Pallas kernels, line_call(): pl.pallas_call(functools.partial(line_kernel, n, groups, CHUNKS, slots),...  102 us
    dot_general x2, matrix products, stored(): lax.dot_general(keep_wide, came, (((0,), (0,)), ((), ())), preferred_elem...  5.41 us
    unnamed x10, local copies, waits for them, and re-layouts  2.89 us

profile of v5, /device:TPU:0, one launch (start us, length us, event | category | flops | bytes accessed | tf_op | source)
XLA Modules:
  0.0 116.1 jit_solution(3432022428627548315)
XLA Ops:
  0.6 0.0 copy-start
  1.3 0.7 broadcast_in_dim.18.live_ref
  2.0 0.7 compare_select_fusion
  2.6 0.0 copy-done
  2.6 0.7 gather_fusion
  3.3 0.1 gather.6
  3.5 0.2 convert_reduce_fusion
  3.7 0.3 fusion.2
  4.0 0.1 mul.40
  4.1 0.1 lt.72
  4.2 0.1 add_select_fusion.1
  4.2 0.1 select_n.61
  4.3 0.8 fusion.5.keep_ref
  5.1 0.1 multiply_reduce_fusion
  5.2 0.1 add_select_fusion
  5.3 0.1 select_n.64
  5.4 0.7 fusion.8.pick_ref
  6.1 101.7 %shard_map.111 = (bf16[960,512]{1,0:T(8,128)(2,1)}, bf16[960,2048]{1,0:T(8,128)(2,1)}, bf16[128,2048]{1,0:T(8,128)(2,1)}, bf16[128,512]{1,0:T(8,128)(2,1)}) custom-call(bf16[960,2048]{1,0:T(8,128)(2,1)} %bitcast.20, bf16[2048,2048]{1,0:T(8,128)(2,1)} %w_hbm.1, bf16[960,512]{1,0:T(8,128)(2,1)} %bitcast.22, f32[8,128]{1,0:T(8,128)} %broadcast_in_dim.18.live_ref, ...), custom_call_target="tpu_custom_call" | custom-call | flops 16106127360 | bytes 30000000 | tf_op jit(solution)/shard_map/pallas_call | solution.py:388
  107.8 0.0 copy-start.3
  107.8 0.0 copy-start.2
  107.8 0.0 copy-start.1
  107.8 4.0 %fusion.4 = f32[512,2048]{1,0:T(8,128)} fusion(bf16[128,2048]{1,0:T(8,128)(2,1)} %get-tuple-element.10, s32[128]{0:T(128)S(1)} %select_n.61), kind=kOutput, calls=%fused_computation.7 | convolution fusion | flops 268500992 | bytes 4719104 | tf_op jit(solution)/shard_map/dot_general | solution.py:499
  111.9 0.0 copy-done.3
  111.9 1.4 %fusion.3 = f32[512,512]{1,0:T(8,128)} fusion(bf16[128,512]{1,0:T(8,128)(2,1)S(1)} %copy-done.3, s32[128]{0:T(128)S(1)} %select_n.61), kind=kOutput, calls=%fused_computation.6 | convolution fusion | flops 67174400 | bytes 1180160 | tf_op jit(solution)/shard_map/dot_general | solution.py:499
  113.3 0.0 copy-done.2
  113.3 0.9 copy.15
  114.2 0.0 copy-done.1
  114.2 1.9 %copy.16 = bf16[8,120,2048]{2,1,0:T(8,128)(2,1)} copy(bf16[8,120,2048]{2,1,0:T(8,128)(2,1)S(1)} %bitcast.17) | data formatting | bytes 7864320
  (14 shorter events, 0.1 us)
Async XLA Ops:
  0.6 2.0 %copy-start = (s32[128]{0:T(128)S(1)}, s32[128]{0:T(128)}, u32[]{:S(2)}) copy-start(s32[128]{0:T(128)} %param.14) | copy-start | bytes 1540
  107.8 4.1 %copy-start.3 = (bf16[128,512]{1,0:T(8,128)(2,1)S(1)}, bf16[128,512]{1,0:T(8,128)(2,1)}, u32[]{:S(2)}) copy-start(bf16[128,512]{1,0:T(8,128)(2,1)} %get-tuple-element.11) | copy-start | bytes 393220
  107.8 5.4 %copy-start.2 = (bf16[960,512]{1,0:T(8,128)(2,1)S(1)}, bf16[960,512]{1,0:T(8,128)(2,1)}, u32[]{:S(2)}) copy-start(bf16[960,512]{1,0:T(8,128)(2,1)} %get-tuple-element.8) | copy-start | bytes 2949124
  107.8 6.4 %copy-start.1 = (bf16[960,2048]{1,0:T(8,128)(2,1)S(1)}, bf16[960,2048]{1,0:T(8,128)(2,1)}, u32[]{:S(2)}) copy-start(bf16[960,2048]{1,0:T(8,128)(2,1)} %get-tuple-element.9) | copy-start | bytes 11796484
